TPU v7x, 128 devices: a whole 4x4x4 slice. The times are simulated.
128 devices in a mesh: seq: 4 (over x), rows: 8 (over z, core), expert: 4 (over y).
Axes of the slice: x: 4, y: 4, z: 4, core: 2. Of those that a mesh axis runs over, the one named last changes fastest.
Arguments:
- queries: bfloat16 [64, 6144], P(('rows', 'expert')), may hold values from -8 to 8
- k_cache: bfloat16 [64, 3072, 1024], P(('rows', 'expert'), 'seq'), may hold values from -12 to 12
- v_cache: bfloat16 [64, 3072, 1024], P(('rows', 'expert'), 'seq'), may hold values from -6 to 6
- k_new: bfloat16 [64, 1024], P(('rows', 'expert')), may hold values from -10 to 10
- v_new: bfloat16 [64, 1024], P(('rows', 'expert')), may hold values from -6 to 6
- lengths: int32 [64], P(('rows', 'expert')), may hold values from 2 to 3072, as said below
- residual: bfloat16 [64, 6144], P(('rows', 'expert')), may hold values from -60 to 60
- norm_gain: float32 [6144], replicated, may hold values from 0.1 to 1.9
- expert_ids: int32 [64, 2], P(('rows', 'expert')), may hold values from 0 to 3, all different within a row; in each aligned block of 2 rows (0 to 1, 2 to 3, ...) at most 2 rows name the same one
- combine_weights: float32 [64, 2], P(('rows', 'expert')), may hold values from 0.2 to 1
- w_gate: bfloat16 [4, 6144, 16384], P('expert', None, ('seq', 'rows')), may hold values from -0.078125 to 0.078125
- w_up: bfloat16 [4, 6144, 16384], P('expert', None, ('seq', 'rows')), may hold values from -0.078125 to 0.078125
- w_down: bfloat16 [4, 16384, 6144], P('expert', ('seq', 'rows')), may hold values from -0.046875 to 0.046875
Outputs:
- hidden_state: bfloat16 [64, 6144], P(('rows', 'expert'), 'seq')
- layer_out: bfloat16 [64, 6144], P(('rows', 'expert'), 'seq')
Inputs may be any that keep to these rules, and one draw needn't show every extreme that they name: `lengths`: the new token is not among them. `expert_ids`: each row names two different experts; within the rows of one group of seq devices (aligned blocks of 2 rows) an expert is named by at most 2 rows.
All inputs are finite; a program needn't handle non-finite values.
Results may differ from a plain program's by a relative error of at most 0.011.
Values may be sent and summed in bfloat16 or wider, within the bound.
No kernel may reach another device: no remote copies, remote signals or barrier semaphores. Data moves between devices by JAX's collectives and lax.ppermute only.
A program may use at most 128 MiB of HBM per device.

v0:
```python
import jax
import jax.numpy as jnp
from jax import lax
from jax.experimental import pallas as pl
from jax.experimental.pallas import tpu as pltpu
from jax.sharding import Mesh, PartitionSpec as P

HEADS = 48
KV_HEADS = 8
EXPERTS = 4
HEAD_DIM = 128
GROUPS = HEADS // KV_HEADS
D = HEADS * HEAD_DIM
SEQ = 4
CTX_HERE = 768
PAY = 112
FF_HERE = 512
BLK = 24
MIB = 1 << 20
NEG = -1e30


def head_masks(shape):
    line = lax.broadcasted_iota(jnp.int32, shape, 0)
    return [(line >= GROUPS * k) & (line < GROUPS * (k + 1)) for k in range(KV_HEADS)]


def spread_heads(row, masks):
    out = jnp.zeros((HEADS, HEAD_DIM), jnp.float32)
    for k in range(KV_HEADS):
        piece = jnp.broadcast_to(row[:, k * HEAD_DIM : (k + 1) * HEAD_DIM], (HEADS, HEAD_DIM))
        out = jnp.where(masks[k], piece, out)
    return out


def attention_kernel(
    len_hbm,
    q_hbm,
    kn_hbm,
    vn_hbm,
    k_hbm,
    v_hbm,
    out_ref,
    len_ref,
    q_ref,
    kn_ref,
    vn_ref,
    kbuf,
    vbuf,
    qs,
    small_sems,
    big_sems,
):
    seq = lax.axis_index("seq")
    sources = ((q_hbm, q_ref), (kn_hbm, kn_ref), (vn_hbm, vn_ref), (len_hbm, len_ref))
    small = [
        pltpu.make_async_copy(src, dst, small_sems.at[i])
        for i, (src, dst) in enumerate(sources)
    ]
    keys = [pltpu.make_async_copy(k_hbm.at[r], kbuf.at[r], big_sems.at[0, r]) for r in range(2)]
    values = [pltpu.make_async_copy(v_hbm.at[r], vbuf.at[r], big_sems.at[1, r]) for r in range(2)]
    small[0].start()
    keys[0].start()
    for copy in small[1:]:
        copy.start()
    keys[1].start()
    factor = HEAD_DIM ** (-0.5)
    masks = head_masks((HEADS, HEAD_DIM))
    line = lax.broadcasted_iota(jnp.int32, (HEADS, HEAD_DIM), 0)
    lane = lax.broadcasted_iota(jnp.int32, (HEADS, HEAD_DIM), 1)
    position = lax.broadcasted_iota(jnp.int32, (HEADS, CTX_HERE), 1) + seq * CTX_HERE
    small[0].wait()
    queries = q_ref[...].astype(jnp.float32)
    for r in range(2):
        for h in range(HEADS):
            qs[r * HEADS + h : r * HEADS + h + 1, :] = queries[
                r : r + 1, h * HEAD_DIM : (h + 1) * HEAD_DIM
            ]
    for copy in small[1:]:
        copy.wait()
    keys_new = kn_ref[...].astype(jnp.float32)
    values_new = vn_ref[...].astype(jnp.float32)
    wides, owns, firsts = [], [], []
    for r in range(2):
        q = qs[r * HEADS : (r + 1) * HEADS, :]
        wides.append(
            jnp.concatenate([jnp.where(m, q, 0.0) for m in masks], axis=1).astype(jnp.bfloat16)
        )
        own = jnp.sum(q * spread_heads(keys_new[r : r + 1], masks), axis=1, keepdims=True) * factor
        owns.append(jnp.where(seq == 0, own, NEG))
        firsts.append(spread_heads(values_new[r : r + 1], masks))
    probs, totals, tops, fresh = [], [], [], []
    for r in range(2):
        keys[r].wait()
        values[r].start()
    for r in range(2):
        scores = (
            lax.dot_general(
                wides[r], kbuf[r], (((1,), (1,)), ((), ())), preferred_element_type=jnp.float32
            )
            * factor
        )
        valid = position < len_ref[r]
        scores = jnp.where(valid, scores, NEG)
        top = jnp.maximum(jnp.max(scores, axis=1, keepdims=True), owns[r])
        weights = jnp.where(valid, jnp.exp(scores - top), 0.0)
        fresh.append(jnp.where(seq == 0, jnp.exp(owns[r] - top), 0.0))
        totals.append(jnp.sum(weights, axis=1, keepdims=True) + fresh[r])
        tops.append(top)
        probs.append(weights.astype(jnp.bfloat16))
    lse_row = jnp.zeros((1, HEAD_DIM), jnp.float32)
    safes = []
    for r in range(2):
        some = totals[r] > 0.0
        safes.append(jnp.where(some, totals[r], 1.0))
        lse = jnp.where(some, tops[r] + jnp.log(safes[r]), NEG)
        lse_row = lse_row + jnp.sum(
            jnp.where(lane == line + r * HEADS, lse, 0.0), axis=0, keepdims=True
        )
    hi = lse_row.astype(jnp.bfloat16).astype(jnp.float32)
    mid = (lse_row - hi).astype(jnp.bfloat16).astype(jnp.float32)
    low = lse_row - hi - mid
    tail = lax.broadcasted_iota(jnp.int32, (16, HEAD_DIM), 0)
    tile = jnp.where(tail == 0, hi, jnp.where(tail == 1, mid, jnp.where(tail == 2, low, 0.0)))
    out_ref[2 * HEADS : PAY, :] = tile.astype(jnp.bfloat16)
    for r in range(2):
        values[r].wait()
        pv = jnp.dot(probs[r], vbuf[r], preferred_element_type=jnp.float32)
        acc = fresh[r] * firsts[r]
        for k in range(KV_HEADS):
            acc = acc + jnp.where(masks[k], pv[:, k * HEAD_DIM : (k + 1) * HEAD_DIM], 0.0)
        out_ref[r * HEADS : (r + 1) * HEADS, :] = (acc / safes[r]).astype(jnp.bfloat16)


def prepare_kernel(
    after, res_hbm, gain_hbm, ids_hbm, cw_hbm, lines_ref, gain_ref, mix_ref, res_ref, ids, cw, sems
):
    pairs = ((res_hbm, res_ref), (gain_hbm, gain_ref), (ids_hbm, ids), (cw_hbm, cw))
    copies = [pltpu.make_async_copy(src, dst, sems.at[i]) for i, (src, dst) in enumerate(pairs)]
    for copy in copies:
        copy.start()
    for copy in copies:
        copy.wait()
    residual = res_ref[...].astype(jnp.float32)
    for r in range(2):
        for h in range(HEADS):
            lines_ref[r * HEADS + h : r * HEADS + h + 1, :] = residual[
                r : r + 1, h * HEAD_DIM : (h + 1) * HEAD_DIM
            ]
    line = lax.broadcasted_iota(jnp.int32, (BLK, HEAD_DIM), 0)
    for e in range(EXPERTS):
        weight = []
        for r in range(2):
            total = 0.0
            for t in range(2):
                total = total + jnp.where(ids[r, t] == e, cw[r, t], 0.0)
            weight.append(total)
        mix_ref[e] = jnp.where(line < BLK // 2, weight[0], weight[1])


def combine_kernel(p0, p1, p2, p3, res_ref, gain_ref, pay_ref, hid_ref, rs):
    seq = lax.axis_index("seq")
    line = lax.broadcasted_iota(jnp.int32, (2 * HEADS, HEAD_DIM), 0)
    lane = lax.broadcasted_iota(jnp.int32, (2 * HEADS, HEAD_DIM), 1)
    lses, outs = [], []
    for ref in (p0, p1, p2, p3):
        outs.append(ref[0 : 2 * HEADS, :].astype(jnp.float32))
        side = ref[2 * HEADS : PAY, :].astype(jnp.float32)
        row = side[0:1, :] + side[1:2, :] + side[2:3, :]
        lses.append(jnp.sum(jnp.where(lane == line, row, 0.0), axis=1, keepdims=True))
    top = jnp.maximum(jnp.maximum(lses[0], lses[1]), jnp.maximum(lses[2], lses[3]))
    scales = [jnp.exp(v - top) for v in lses]
    total = (scales[0] + scales[1]) + (scales[2] + scales[3])
    acc = (scales[0] * outs[0] + scales[1] * outs[1]) + (scales[2] * outs[2] + scales[3] * outs[3])
    hidden = (res_ref[...] + acc / total).astype(jnp.bfloat16).astype(jnp.float32)
    rs[...] = hidden
    normed = []
    for r in range(2):
        x = hidden[r * HEADS : (r + 1) * HEADS, :]
        square = jnp.sum(jnp.sum(x * x, axis=0, keepdims=True), axis=1, keepdims=True)
        normed.append(x * lax.rsqrt(square * (1.0 / D) + 1e-05) * gain_ref[...])
    normed = jnp.concatenate(normed, axis=0).astype(jnp.bfloat16)
    for j in range(16):
        pay_ref[j] = normed
    rows = []
    for r in range(2):
        first = r * HEADS + seq * (HEADS // SEQ)
        rows.append(
            jnp.concatenate([rs[pl.ds(first + c, 1), :] for c in range(HEADS // SEQ)], axis=1)
        )
    hid_ref[...] = jnp.concatenate(rows, axis=0).astype(jnp.bfloat16)


def expert_kernel(xa, xb, wg, wu, wd, own_ref, sib_ref, flat, lhs):
    parts = 6
    kc = D // parts
    for half, ref in enumerate((xa, xb)):
        for j in range(16):
            row = half * 32 + 2 * j
            flat[row * HEADS : (row + 2) * HEADS, :] = ref[j].astype(jnp.float32)
    for h in range(HEADS):
        x = flat[pl.ds(h, 64, stride=HEADS), :]
        lhs[:, h * HEAD_DIM : (h + 1) * HEAD_DIM] = x.astype(jnp.bfloat16)
    gate = jnp.zeros((64, FF_HERE), jnp.float32)
    upper = jnp.zeros((64, FF_HERE), jnp.float32)
    for i in range(parts):
        x = lhs[:, i * kc : (i + 1) * kc]
        gate = gate + jnp.dot(x, wg[0, i * kc : (i + 1) * kc, :], preferred_element_type=jnp.float32)
        upper = upper + jnp.dot(x, wu[0, i * kc : (i + 1) * kc, :], preferred_element_type=jnp.float32)
    act = (gate / (1.0 + jnp.exp(-gate)) * upper).astype(jnp.bfloat16)
    for i in range(parts):
        out = jnp.dot(act, wd[0, :, i * kc : (i + 1) * kc], preferred_element_type=jnp.float32)
        for g in range(kc // HEAD_DIM):
            place = i * (kc // HEAD_DIM) + g
            piece = out[:, g * HEAD_DIM : (g + 1) * HEAD_DIM]
            first = (place // 12) * (16 * BLK) + place % 12
            flat[pl.ds(first, 32, stride=12), :] = piece[0:32]
            flat[pl.ds(64 * BLK + first, 32, stride=12), :] = piece[32:64]
    own_ref[...] = flat[0 : 64 * BLK, :].astype(jnp.bfloat16)
    sib_ref[...] = flat[64 * BLK : 128 * BLK, :].astype(jnp.bfloat16)


def finish_kernel(parts_ref, mix_ref, hid_ref, out_ref, hid_out):
    hid_out[...] = hid_ref[...]
    total = jnp.zeros((BLK, HEAD_DIM), jnp.float32)
    for e in range(EXPERTS):
        group = jnp.zeros((BLK, HEAD_DIM), jnp.float32)
        for j in range(64 // EXPERTS):
            group = group + parts_ref[j * EXPERTS + e].astype(jnp.float32)
        total = total + group * mix_ref[e]
    rows = [
        jnp.concatenate([total[r * 12 + c : r * 12 + c + 1, :] for c in range(12)], axis=1)
        for r in range(2)
    ]
    mixture = jnp.concatenate(rows, axis=0)
    out_ref[...] = (hid_ref[...].astype(jnp.float32) + mixture).astype(jnp.bfloat16)


VMEM = pl.BlockSpec(memory_space=pltpu.VMEM)
HBM = pl.BlockSpec(memory_space=pltpu.HBM)


def params(mib):
    return pltpu.CompilerParams(vmem_limit_bytes=mib * MIB)


def body(
    queries,
    k_cache,
    v_cache,
    k_new,
    v_new,
    lengths,
    residual,
    norm_gain,
    expert_ids,
    combine_weights,
    w_gate,
    w_up,
    w_down,
):
    bf16, f32 = jnp.bfloat16, jnp.float32
    partial = pl.pallas_call(
        attention_kernel,
        out_shape=pltpu.VMEM((PAY, HEAD_DIM), bf16),
        in_specs=[HBM] * 6,
        out_specs=VMEM,
        scratch_shapes=[
            pltpu.SMEM((2,), jnp.int32),
            pltpu.VMEM((2, D), bf16),
            pltpu.VMEM((2, KV_HEADS * HEAD_DIM), bf16),
            pltpu.VMEM((2, KV_HEADS * HEAD_DIM), bf16),
            pltpu.VMEM((2, CTX_HERE, KV_HEADS * HEAD_DIM), bf16),
            pltpu.VMEM((2, CTX_HERE, KV_HEADS * HEAD_DIM), bf16),
            pltpu.VMEM((2 * HEADS, HEAD_DIM), f32),
            pltpu.SemaphoreType.DMA((4,)),
            pltpu.SemaphoreType.DMA((2, 2)),
        ],
        compiler_params=params(58),
        name="attention",
    )(lengths, queries, k_new, v_new, k_cache, v_cache)
    residual_lines, gain_lines, mix_lines = pl.pallas_call(
        prepare_kernel,
        out_shape=(
            pltpu.VMEM((2 * HEADS, HEAD_DIM), f32),
            pltpu.VMEM((HEADS, HEAD_DIM), f32),
            pltpu.VMEM((EXPERTS, BLK, HEAD_DIM), f32),
        ),
        in_specs=[pl.BlockSpec(memory_space=pl.ANY)] + [HBM] * 4,
        out_specs=(VMEM, VMEM, VMEM),
        scratch_shapes=[
            pltpu.VMEM((2, D), bf16),
            pltpu.SMEM((2, 2), jnp.int32),
            pltpu.SMEM((2, 2), f32),
            pltpu.SemaphoreType.DMA((4,)),
        ],
        compiler_params=params(8),
        name="prepare",
    )(partial, residual, norm_gain.reshape(HEADS, HEAD_DIM), expert_ids, combine_weights)
    others = [
        lax.ppermute(partial, "seq", [(i, (i + k) % SEQ) for i in range(SEQ)]) for k in (1, 3, 2)
    ]
    pay, hidden_part = pl.pallas_call(
        combine_kernel,
        out_shape=(
            pltpu.VMEM((16, 2 * HEADS, HEAD_DIM), bf16),
            pltpu.VMEM((2, D // SEQ), bf16),
        ),
        in_specs=[VMEM] * 6,
        out_specs=(VMEM, VMEM),
        scratch_shapes=[pltpu.VMEM((2 * HEADS, HEAD_DIM), f32)],
        compiler_params=params(8),
        cost_estimate=pl.CostEstimate(
            flops=2_000_000_000_000, bytes_accessed=6_000_000_000, transcendentals=0
        ),
        name="combine",
    )(partial, *others, residual_lines, gain_lines)
    mine = lax.all_to_all(pay, ("z", "expert"), 0, 0, tiled=True)
    theirs = lax.ppermute(mine, "core", [(0, 1), (1, 0)])
    own_out, sib_out = pl.pallas_call(
        expert_kernel,
        out_shape=(
            jax.ShapeDtypeStruct((64 * BLK, HEAD_DIM), bf16),
            jax.ShapeDtypeStruct((64 * BLK, HEAD_DIM), bf16),
        ),
        in_specs=[VMEM] * 5,
        out_specs=(VMEM, VMEM),
        scratch_shapes=[
            pltpu.VMEM((64 * HEADS, HEAD_DIM), f32),
            pltpu.VMEM((64, D), bf16),
        ],
        compiler_params=params(8),
        name="experts",
    )(mine, theirs, w_gate, w_up, w_down)
    from_sib = lax.ppermute(sib_out, "core", [(0, 1), (1, 0)])
    summed = (own_out.astype(f32) + from_sib.astype(f32)).astype(bf16)
    blocks = lax.all_to_all(
        summed.reshape(64, BLK, HEAD_DIM), ("seq", "z", "expert"), 0, 0, tiled=True
    )
    layer_out, hidden_out = pl.pallas_call(
        finish_kernel,
        out_shape=(jax.ShapeDtypeStruct((2, D // SEQ), bf16),) * 2,
        in_specs=[VMEM] * 3,
        out_specs=(VMEM, VMEM),
        compiler_params=params(8),
        name="finish",
    )(blocks, mix_lines, hidden_part)
    return hidden_out, layer_out


def solution(mesh):
    fine = Mesh(mesh.devices.reshape(4, 4, 2, 4), ("seq", "z", "core", "expert"))
    rows = ("z", "core", "expert")
    in_specs = (
        P(rows, None),
        P(rows, "seq", None),
        P(rows, "seq", None),
        P(rows, None),
        P(rows, None),
        P(rows),
        P(rows, None),
        P(),
        P(rows, None),
        P(rows, None),
        P("expert", None, ("seq", "z", "core")),
        P("expert", None, ("seq", "z", "core")),
        P("expert", ("seq", "z", "core"), None),
    )
    out_specs = (P(rows, "seq"), P(rows, "seq"))
    return jax.shard_map(body, mesh=fine, in_specs=in_specs, out_specs=out_specs, check_vma=False)
```

profile of v0, /device:TPU:0, one launch (start us, length us, event | category | flops | bytes accessed | tf_op | source)
XLA Modules:
  0.0 56.0 jit_solution(8186372589681266465)
XLA Ops:
  0.6 0.0 copy-start.6
  0.6 0.0 copy-start.5
  0.7 0.0 copy-start.4
  0.7 0.0 copy-start.3
  0.7 4.1 %attention.1.after.p0 = bf16[112,128]{1,0:T(8,128)(2,1)S(1)} custom-call(s32[2]{0:T(128)} %len_hbm.1, bf16[2,6144]{1,0:T(2,128)(2,1)} %q_hbm.1, bf16[2,1024]{1,0:T(2,128)(2,1)} %kn_hbm.1, bf16[2,1024]{1,0:T(2,128)(2,1)} %vn_hbm.1, bf16[2,768,1024]{2,1,0:T(8,128)(2,1)} %k_hbm.1, bf16[2,768,1024]{2,1,0:T(8,128)(2,1)} %v_hbm.1), custom_call_target="tpu_custom_call" | custom-call | tf_op jit(solution)/shard_map/attention/pallas_call | solution.py:263
  4.7 3.2 %collective-permute-start.2 = (bf16[112,128]{1,0:T(8,128)(2,1)S(1)}, bf16[112,128]{1,0:T(8,128)(2,1)S(1)}, u32[]{:S(2)}, u32[]{:S(2)}) collective-permute-start(bf16[112,128]{1,0:T(8,128)(2,1)S(1)} %attention.1.after.p0), channel_id=1, source_target_pairs={{0,64},{32,96},{64,0},{96,32},{1,65},{33,97},{65,1},{97,33},{2,66}... | collective-permute-start | bytes 86024 | tf_op jit(solution)/shard_map/ppermute | solution.py:301
  7.9 1.1 %collective-permute-start.1 = (bf16[112,128]{1,0:T(8,128)(2,1)S(1)}, bf16[112,128]{1,0:T(8,128)(2,1)S(1)}, u32[]{:S(2)}, u32[]{:S(2)}) collective-permute-start(bf16[112,128]{1,0:T(8,128)(2,1)S(1)} %attention.1.after.p0), channel_id=1, source_target_pairs={{0,96},{32,0},{64,32},{96,64},{1,97},{33,1},{65,33},{97,65},{2,98}... | collective-permute-start | bytes 86024 | tf_op jit(solution)/shard_map/ppermute | solution.py:301
  9.1 0.9 %collective-permute-start = (bf16[112,128]{1,0:T(8,128)(2,1)S(1)}, bf16[112,128]{1,0:T(8,128)(2,1)S(1)}, u32[]{:S(2)}, u32[]{:S(2)}) collective-permute-start(bf16[112,128]{1,0:T(8,128)(2,1)S(1)} %attention.1.after.p0), channel_id=1, source_target_pairs={{0,32},{32,64},{64,96},{96,0},{1,33},{33,65},{65,97},{97,1},{2,34}... | collective-permute-start | bytes 86024 | tf_op jit(solution)/shard_map/ppermute | solution.py:301
  10.0 0.0 copy-done.6
  10.0 0.0 copy-done.5
  10.0 0.0 copy-done.4
  10.0 0.0 copy-done.3
  10.0 0.7 %prepare.1 = (f32[96,128]{1,0:T(8,128)S(1)}, f32[48,128]{1,0:T(8,128)S(1)}, f32[4,24,128]{2,1,0:T(8,128)S(1)}) custom-call(bf16[112,128]{1,0:T(8,128)(2,1)S(1)} %attention.1.after.p0, bf16[2,6144]{1,0:T(2,128)(2,1)S(1)} %copy-done.3, f32[48,128]{1,0:T(8,128)S(1)} %bitcast.2, s32[2,2]{1,0:T(2,128)S(1)} %copy-done.5, f32[2,2]{1,0:T(2,128)S(1)} %copy-done.6), custom_call_target="tpu_custom_call" | custom-call | tf_op jit(solution)/shard_map/prepare/pallas_call | solution.py:282
  10.7 0.0 collective-permute-done.2.p3
  10.7 1.1 %collective-permute-done.1.p2 = bf16[112,128]{1,0:T(8,128)(2,1)S(1)} collective-permute-done((bf16[112,128]{1,0:T(8,128)(2,1)S(1)}, bf16[112,128]{1,0:T(8,128)(2,1)S(1)}, u32[]{:S(2)}, u32[]{:S(2)}) %collective-permute-start.1) | collective-permute-done | bytes 28704 | tf_op jit(solution)/shard_map/ppermute | solution.py:301
  11.8 2.4 %collective-permute-done.p1 = bf16[112,128]{1,0:T(8,128)(2,1)S(1)} collective-permute-done((bf16[112,128]{1,0:T(8,128)(2,1)S(1)}, bf16[112,128]{1,0:T(8,128)(2,1)S(1)}, u32[]{:S(2)}, u32[]{:S(2)}) %collective-permute-start) | collective-permute-done | bytes 28704 | tf_op jit(solution)/shard_map/ppermute | solution.py:301
  14.2 0.0 copy-start
  14.2 0.0 copy-start.1
  14.2 0.0 copy-start.2
  14.2 0.3 combine.1
  14.4 17.5 %all_to_all.10.xa = bf16[16,96,128]{2,1,0:T(8,128)(2,1)S(1)} all-to-all(bf16[16,96,128]{2,1,0:T(8,128)(2,1)S(1)} %get-tuple-element.13), channel_id=1, replica_groups=mesh['seq'=4,'z'=4,'core'=2,'expert'=4] {'z','expert'}, dimensions={0} | all-to-all | bytes 786432 | tf_op jit(solution)/shard_map/all_to_all | solution.py:318
  32.0 0.0 collective-permute-start.3
  32.0 1.7 %collective-permute-done.3.xb = bf16[16,96,128]{2,1,0:T(8,128)(2,1)S(1)} collective-permute-done((bf16[16,96,128]{2,1,0:T(8,128)(2,1)S(1)}, bf16[16,96,128]{2,1,0:T(8,128)(2,1)S(1)}, u32[]{:S(2)}, u32[]{:S(2)}) %collective-permute-start.3) | collective-permute-done | bytes 393248 | tf_op jit(solution)/shard_map/ppermute | solution.py:319
  33.7 0.0 copy-done
  33.7 0.0 copy-done.1
  33.7 0.0 copy-done.2
  33.7 3.6 %experts.1 = (bf16[1536,128]{1,0:T(8,128)(2,1)S(1)}, bf16[1536,128]{1,0:T(8,128)(2,1)S(1)}) custom-call(bf16[16,96,128]{2,1,0:T(8,128)(2,1)S(1)} %all_to_all.10.xa, bf16[16,96,128]{2,1,0:T(8,128)(2,1)S(1)} %collective-permute-done.3.xb, bf16[1,6144,512]{2,1,0:T(8,128)(2,1)S(1)} %copy-done, bf16[1,6144,512]{2,1,0:T(8,128)(2,1)S(1)} %copy-done.1, ...), custom_call_target="tpu_custom_call" | custom-call | tf_op jit(solution)/shard_map/experts/pallas_call | solution.py:320
  37.3 0.2 collective-permute-start.4
  37.5 1.6 %collective-permute-done.4 = bf16[1536,128]{1,0:T(8,128)(2,1)S(1)} collective-permute-done((bf16[1536,128]{1,0:T(8,128)(2,1)S(1)}, bf16[1536,128]{1,0:T(8,128)(2,1)S(1)}, u32[]{:S(2)}, u32[]{:S(2)}) %collective-permute-start.4) | collective-permute-done | bytes 393248 | tf_op jit(solution)/shard_map/ppermute | solution.py:335
  39.1 0.1 add_convert_fusion
  39.2 16.2 %all_to_all.11.parts_ref = bf16[64,24,128]{2,1,0:T(8,128)(2,1)S(1)} all-to-all(bf16[64,24,128]{2,1,0:T(8,128)(2,1)S(1)} %bitcast.3), channel_id=1, replica_groups=mesh['seq'=4,'z'=4,'core'=2,'expert'=4] {'seq','z','expert'}, dimensions={0} | all-to-all | bytes 786432 | tf_op jit(solution)/shard_map/all_to_all | solution.py:337
  55.4 0.7 %finish.1 = (bf16[2,1536]{1,0:T(2,128)(2,1)}, bf16[2,1536]{1,0:T(2,128)(2,1)}) custom-call(bf16[64,24,128]{2,1,0:T(8,128)(2,1)S(1)} %all_to_all.11.parts_ref, f32[4,24,128]{2,1,0:T(8,128)S(1)} %get-tuple-element.16.mix_ref, bf16[2,1536]{1,0:T(2,128)(2,1)S(1)} %get-tuple-element.17.hid_ref), custom_call_target="tpu_custom_call" | custom-call | tf_op jit(solution)/shard_map/finish/pallas_call | solution.py:340
Async XLA Ops:
  0.6 9.3 %copy-start.6 = (f32[2,2]{1,0:T(2,128)S(1)}, f32[2,2]{1,0:T(2,128)}, u32[]{:S(2)}) copy-start(f32[2,2]{1,0:T(2,128)} %cw_hbm.1) | copy-start | bytes 52
  0.6 9.3 %copy-start.5 = (s32[2,2]{1,0:T(2,128)S(1)}, s32[2,2]{1,0:T(2,128)}, u32[]{:S(2)}) copy-start(s32[2,2]{1,0:T(2,128)} %ids_hbm.1) | copy-start | bytes 52
  0.7 9.3 %copy-start.4 = (f32[6144]{0:T(1024)S(1)}, f32[6144]{0:T(1024)}, u32[]{:S(2)}) copy-start(f32[6144]{0:T(1024)} %param.20) | copy-start | bytes 73732
  0.7 9.3 %copy-start.3 = (bf16[2,6144]{1,0:T(2,128)(2,1)S(1)}, bf16[2,6144]{1,0:T(2,128)(2,1)}, u32[]{:S(2)}) copy-start(bf16[2,6144]{1,0:T(2,128)(2,1)} %res_hbm.1) | copy-start | bytes 73732
  4.7 5.9 %collective-permute-start.2 = (bf16[112,128]{1,0:T(8,128)(2,1)S(1)}, bf16[112,128]{1,0:T(8,128)(2,1)S(1)}, u32[]{:S(2)}, u32[]{:S(2)}) collective-permute-start(bf16[112,128]{1,0:T(8,128)(2,1)S(1)} %attention.1.after.p0), channel_id=1, source_target_pairs={{0,64},{32,96},{64,0},{96,32},{1,65},{33,97},{65,1},{97,33},{2,66}... | collective-permute-start | bytes 86024 | tf_op jit(solution)/shard_map/ppermute | solution.py:301
  7.9 3.9 %collective-permute-start.1 = (bf16[112,128]{1,0:T(8,128)(2,1)S(1)}, bf16[112,128]{1,0:T(8,128)(2,1)S(1)}, u32[]{:S(2)}, u32[]{:S(2)}) collective-permute-start(bf16[112,128]{1,0:T(8,128)(2,1)S(1)} %attention.1.after.p0), channel_id=1, source_target_pairs={{0,96},{32,0},{64,32},{96,64},{1,97},{33,1},{65,33},{97,65},{2,98}... | collective-permute-start | bytes 86024 | tf_op jit(solution)/shard_map/ppermute | solution.py:301
  9.1 5.1 %collective-permute-start = (bf16[112,128]{1,0:T(8,128)(2,1)S(1)}, bf16[112,128]{1,0:T(8,128)(2,1)S(1)}, u32[]{:S(2)}, u32[]{:S(2)}) collective-permute-start(bf16[112,128]{1,0:T(8,128)(2,1)S(1)} %attention.1.after.p0), channel_id=1, source_target_pairs={{0,32},{32,64},{64,96},{96,0},{1,33},{33,65},{65,97},{97,1},{2,34}... | collective-permute-start | bytes 86024 | tf_op jit(solution)/shard_map/ppermute | solution.py:301
  14.2 19.5 %copy-start = (bf16[1,6144,512]{2,1,0:T(8,128)(2,1)S(1)}, bf16[1,6144,512]{2,1,0:T(8,128)(2,1)}, u32[]{:S(2)}) copy-start(bf16[1,6144,512]{2,1,0:T(8,128)(2,1)} %wg.1) | copy-start | bytes 18874372
  14.2 19.5 %copy-start.1 = (bf16[1,6144,512]{2,1,0:T(8,128)(2,1)S(1)}, bf16[1,6144,512]{2,1,0:T(8,128)(2,1)}, u32[]{:S(2)}) copy-start(bf16[1,6144,512]{2,1,0:T(8,128)(2,1)} %wu.1) | copy-start | bytes 18874372
  14.2 19.5 %copy-start.2 = (bf16[1,512,6144]{2,1,0:T(8,128)(2,1)S(1)}, bf16[1,512,6144]{2,1,0:T(8,128)(2,1)}, u32[]{:S(2)}) copy-start(bf16[1,512,6144]{2,1,0:T(8,128)(2,1)} %wd.1) | copy-start | bytes 18874372
  32.0 1.7 %collective-permute-start.3 = (bf16[16,96,128]{2,1,0:T(8,128)(2,1)S(1)}, bf16[16,96,128]{2,1,0:T(8,128)(2,1)S(1)}, u32[]{:S(2)}, u32[]{:S(2)}) collective-permute-start(bf16[16,96,128]{2,1,0:T(8,128)(2,1)S(1)} %all_to_all.10.xa), channel_id=1, source_target_pairs={{0,4},{4,0},{1,5},{5,1},{2,6},{6,2},{3,7},{7,3},{8,12},{12,8},{9,1... | collective-permute-start | bytes 1179656 | tf_op jit(solution)/shard_map/ppermute | solution.py:319
  37.3 1.8 %collective-permute-start.4 = (bf16[1536,128]{1,0:T(8,128)(2,1)S(1)}, bf16[1536,128]{1,0:T(8,128)(2,1)S(1)}, u32[]{:S(2)}, u32[]{:S(2)}) collective-permute-start(bf16[1536,128]{1,0:T(8,128)(2,1)S(1)} %get-tuple-element.15), channel_id=1, source_target_pairs={{0,4},{4,0},{1,5},{5,1},{2,6},{6,2},{3,7},{7,3},{8,12},{12,8},{9,1... | collective-permute-start | bytes 1179656 | tf_op jit(solution)/shard_map/ppermute | solution.py:335
where the time goes:
time: 56.2 us; the launch traced here: 56 us
  blocking collectives  33.7 us (60%)
  Pallas kernels  9.29 us (17%)
  waiting for transfers between devices  6.77 us (12%)
  starting transfers between devices  5.43 us (10%)
  between operations  0.72 us (1%)
    all_to_all x1, blocking collectives, body(): mine = lax.all_to_all(pay, ('z', 'expert'), 0, 0, tiled=True)  17.5 us
    all_to_all x1, blocking collectives, body(): lax.all_to_all(summed.reshape(64, BLK, HEAD_DIM), ('seq', 'z', 'expert'),...  16.2 us
    ppermute x3, starting transfers between devices, body(): lax.ppermute(partial, 'seq', [(i, (i + k) % SEQ) for i in range(SEQ)])  5.21 us
    pallas_call x1, Pallas kernels, body(): pl.pallas_call(attention_kernel, out_shape=pltpu.VMEM((PAY, HEAD_DIM), bf...  4.07 us
    pallas_call x1, Pallas kernels, body(): pl.pallas_call(expert_kernel, out_shape=(jax.ShapeDtypeStruct((64 * BLK,...  3.57 us
    ppermute x3, waiting for transfers between devices, body(): lax.ppermute(partial, 'seq', [(i, (i + k) % SEQ) for i in range(SEQ)])  3.46 us
    ppermute x1, waiting for transfers between devices, body(): theirs = lax.ppermute(mine, 'core', [(0, 1), (1, 0)])  1.72 us
    ppermute x1, waiting for transfers between devices, body(): from_sib = lax.ppermute(sib_out, 'core', [(0, 1), (1, 0)])  1.59 us
  transfers between devices with their start and end apart: 5, of which 4 were waited for; matrix products, arithmetic and copies ran while one was open for 0% of the time, Pallas kernels for 1%

commit v1 on v0

--- a/solution.py
+++ b/solution.py
@@ -63,7 +63,8 @@
     keys[0].start()
     for copy in small[1:]:
         copy.start()
-    keys[1].start()
+    for copy in keys[1:] + values:
+        copy.start(priority=1)
     factor = HEAD_DIM ** (-0.5)
     masks = head_masks((HEADS, HEAD_DIM))
     line = lax.broadcasted_iota(jnp.int32, (HEADS, HEAD_DIM), 0)
@@ -89,21 +90,20 @@
         own = jnp.sum(q * spread_heads(keys_new[r : r + 1], masks), axis=1, keepdims=True) * factor
         owns.append(jnp.where(seq == 0, own, NEG))
         firsts.append(spread_heads(values_new[r : r + 1], masks))
-    probs, totals, tops, fresh = [], [], [], []
+    scores = []
     for r in range(2):
         keys[r].wait()
-        values[r].start()
-    for r in range(2):
-        scores = (
+        scores.append(
             lax.dot_general(
                 wides[r], kbuf[r], (((1,), (1,)), ((), ())), preferred_element_type=jnp.float32
             )
-            * factor
         )
+    probs, totals, tops, fresh = [], [], [], []
+    for r in range(2):
         valid = position < len_ref[r]
-        scores = jnp.where(valid, scores, NEG)
-        top = jnp.maximum(jnp.max(scores, axis=1, keepdims=True), owns[r])
-        weights = jnp.where(valid, jnp.exp(scores - top), 0.0)
+        score = jnp.where(valid, scores[r] * factor, NEG)
+        top = jnp.maximum(jnp.max(score, axis=1, keepdims=True), owns[r])
+        weights = jnp.where(valid, jnp.exp(score - top), 0.0)
         fresh.append(jnp.where(seq == 0, jnp.exp(owns[r] - top), 0.0))
         totals.append(jnp.sum(weights, axis=1, keepdims=True) + fresh[r])
         tops.append(top)
@@ -123,8 +123,9 @@
     tail = lax.broadcasted_iota(jnp.int32, (16, HEAD_DIM), 0)
     tile = jnp.where(tail == 0, hi, jnp.where(tail == 1, mid, jnp.where(tail == 2, low, 0.0)))
     out_ref[2 * HEADS : PAY, :] = tile.astype(jnp.bfloat16)
-    for r in range(2):
-        values[r].wait()
+    for copy in values:
+        copy.wait()
+    for r in range(2):
         pv = jnp.dot(probs[r], vbuf[r], preferred_element_type=jnp.float32)
         acc = fresh[r] * firsts[r]
         for k in range(KV_HEADS):

time: 56.2 us -> 55.9 us (level)
  no operation moved by 1% of the time
where the time goes in v1:
time: 55.9 us; the launch traced here: 55.7 us
  blocking collectives  33.7 us (60%)
  Pallas kernels  9.01 us (16%)
  waiting for transfers between devices  6.77 us (12%)
  starting transfers between devices  5.42 us (10%)
  between operations  0.72 us (1%)
    all_to_all x1, blocking collectives, body(): mine = lax.all_to_all(pay, ('z', 'expert'), 0, 0, tiled=True)  17.5 us
    all_to_all x1, blocking collectives, body(): lax.all_to_all(summed.reshape(64, BLK, HEAD_DIM), ('seq', 'z', 'expert'),...  16.2 us
    ppermute x3, starting transfers between devices, body(): lax.ppermute(partial, 'seq', [(i, (i + k) % SEQ) for i in range(SEQ)])  5.21 us
    pallas_call x1, Pallas kernels, body(): pl.pallas_call(attention_kernel, out_shape=pltpu.VMEM((PAY, HEAD_DIM), bf...  3.8 us
    pallas_call x1, Pallas kernels, body(): pl.pallas_call(expert_kernel, out_shape=(jax.ShapeDtypeStruct((64 * BLK,...  3.57 us
    ppermute x3, waiting for transfers between devices, body(): lax.ppermute(partial, 'seq', [(i, (i + k) % SEQ) for i in range(SEQ)])  3.46 us
    ppermute x1, waiting for transfers between devices, body(): theirs = lax.ppermute(mine, 'core', [(0, 1), (1, 0)])  1.72 us
    ppermute x1, waiting for transfers between devices, body(): from_sib = lax.ppermute(sib_out, 'core', [(0, 1), (1, 0)])  1.59 us
  transfers between devices with their start and end apart: 5, of which 4 were waited for; matrix products, arithmetic and copies ran while one was open for 0% of the time, Pallas kernels for 1%

profile of v1, /device:TPU:0, one launch (start us, length us, event | category | flops | bytes accessed | tf_op | source)
XLA Modules:
  0.0 55.7 jit_solution(1220089095759421818)
XLA Ops:
  0.6 0.0 copy-start.6
  0.6 0.0 copy-start.5
  0.7 0.0 copy-start.4
  0.7 0.0 copy-start.3
  0.7 3.8 %attention.1.after.p0 = bf16[112,128]{1,0:T(8,128)(2,1)S(1)} custom-call(s32[2]{0:T(128)} %len_hbm.1, bf16[2,6144]{1,0:T(2,128)(2,1)} %q_hbm.1, bf16[2,1024]{1,0:T(2,128)(2,1)} %kn_hbm.1, bf16[2,1024]{1,0:T(2,128)(2,1)} %vn_hbm.1, bf16[2,768,1024]{2,1,0:T(8,128)(2,1)} %k_hbm.1, bf16[2,768,1024]{2,1,0:T(8,128)(2,1)} %v_hbm.1), custom_call_target="tpu_custom_call" | custom-call | tf_op jit(solution)/shard_map/attention/pallas_call | solution.py:264
  4.5 3.2 %collective-permute-start.2 = (bf16[112,128]{1,0:T(8,128)(2,1)S(1)}, bf16[112,128]{1,0:T(8,128)(2,1)S(1)}, u32[]{:S(2)}, u32[]{:S(2)}) collective-permute-start(bf16[112,128]{1,0:T(8,128)(2,1)S(1)} %attention.1.after.p0), channel_id=1, source_target_pairs={{0,64},{32,96},{64,0},{96,32},{1,65},{33,97},{65,1},{97,33},{2,66}... | collective-permute-start | bytes 86024 | tf_op jit(solution)/shard_map/ppermute | solution.py:302
  7.7 1.1 %collective-permute-start.1 = (bf16[112,128]{1,0:T(8,128)(2,1)S(1)}, bf16[112,128]{1,0:T(8,128)(2,1)S(1)}, u32[]{:S(2)}, u32[]{:S(2)}) collective-permute-start(bf16[112,128]{1,0:T(8,128)(2,1)S(1)} %attention.1.after.p0), channel_id=1, source_target_pairs={{0,96},{32,0},{64,32},{96,64},{1,97},{33,1},{65,33},{97,65},{2,98}... | collective-permute-start | bytes 86024 | tf_op jit(solution)/shard_map/ppermute | solution.py:302
  8.8 0.9 %collective-permute-start = (bf16[112,128]{1,0:T(8,128)(2,1)S(1)}, bf16[112,128]{1,0:T(8,128)(2,1)S(1)}, u32[]{:S(2)}, u32[]{:S(2)}) collective-permute-start(bf16[112,128]{1,0:T(8,128)(2,1)S(1)} %attention.1.after.p0), channel_id=1, source_target_pairs={{0,32},{32,64},{64,96},{96,0},{1,33},{33,65},{65,97},{97,1},{2,34}... | collective-permute-start | bytes 86024 | tf_op jit(solution)/shard_map/ppermute | solution.py:302
  9.7 0.0 copy-done.6
  9.7 0.0 copy-done.5
  9.7 0.0 copy-done.4
  9.7 0.0 copy-done.3
  9.7 0.7 %prepare.1 = (f32[96,128]{1,0:T(8,128)S(1)}, f32[48,128]{1,0:T(8,128)S(1)}, f32[4,24,128]{2,1,0:T(8,128)S(1)}) custom-call(bf16[112,128]{1,0:T(8,128)(2,1)S(1)} %attention.1.after.p0, bf16[2,6144]{1,0:T(2,128)(2,1)S(1)} %copy-done.3, f32[48,128]{1,0:T(8,128)S(1)} %bitcast.2, s32[2,2]{1,0:T(2,128)S(1)} %copy-done.5, f32[2,2]{1,0:T(2,128)S(1)} %copy-done.6), custom_call_target="tpu_custom_call" | custom-call | tf_op jit(solution)/shard_map/prepare/pallas_call | solution.py:283
  10.4 0.0 collective-permute-done.2.p3
  10.4 1.1 %collective-permute-done.1.p2 = bf16[112,128]{1,0:T(8,128)(2,1)S(1)} collective-permute-done((bf16[112,128]{1,0:T(8,128)(2,1)S(1)}, bf16[112,128]{1,0:T(8,128)(2,1)S(1)}, u32[]{:S(2)}, u32[]{:S(2)}) %collective-permute-start.1) | collective-permute-done | bytes 28704 | tf_op jit(solution)/shard_map/ppermute | solution.py:302
  11.5 2.4 %collective-permute-done.p1 = bf16[112,128]{1,0:T(8,128)(2,1)S(1)} collective-permute-done((bf16[112,128]{1,0:T(8,128)(2,1)S(1)}, bf16[112,128]{1,0:T(8,128)(2,1)S(1)}, u32[]{:S(2)}, u32[]{:S(2)}) %collective-permute-start) | collective-permute-done | bytes 28704 | tf_op jit(solution)/shard_map/ppermute | solution.py:302
  13.9 0.0 copy-start
  13.9 0.0 copy-start.1
  13.9 0.0 copy-start.2
  13.9 0.3 combine.1
  14.2 17.5 %all_to_all.10.xa = bf16[16,96,128]{2,1,0:T(8,128)(2,1)S(1)} all-to-all(bf16[16,96,128]{2,1,0:T(8,128)(2,1)S(1)} %get-tuple-element.13), channel_id=1, replica_groups=mesh['seq'=4,'z'=4,'core'=2,'expert'=4] {'z','expert'}, dimensions={0} | all-to-all | bytes 786432 | tf_op jit(solution)/shard_map/all_to_all | solution.py:319
  31.7 0.0 collective-permute-start.3
  31.7 1.7 %collective-permute-done.3.xb = bf16[16,96,128]{2,1,0:T(8,128)(2,1)S(1)} collective-permute-done((bf16[16,96,128]{2,1,0:T(8,128)(2,1)S(1)}, bf16[16,96,128]{2,1,0:T(8,128)(2,1)S(1)}, u32[]{:S(2)}, u32[]{:S(2)}) %collective-permute-start.3) | collective-permute-done | bytes 393248 | tf_op jit(solution)/shard_map/ppermute | solution.py:320
  33.4 0.0 copy-done
  33.4 0.0 copy-done.1
  33.4 0.0 copy-done.2
  33.4 3.6 %experts.1 = (bf16[1536,128]{1,0:T(8,128)(2,1)S(1)}, bf16[1536,128]{1,0:T(8,128)(2,1)S(1)}) custom-call(bf16[16,96,128]{2,1,0:T(8,128)(2,1)S(1)} %all_to_all.10.xa, bf16[16,96,128]{2,1,0:T(8,128)(2,1)S(1)} %collective-permute-done.3.xb, bf16[1,6144,512]{2,1,0:T(8,128)(2,1)S(1)} %copy-done, bf16[1,6144,512]{2,1,0:T(8,128)(2,1)S(1)} %copy-done.1, ...), custom_call_target="tpu_custom_call" | custom-call | tf_op jit(solution)/shard_map/experts/pallas_call | solution.py:321
  37.0 0.2 collective-permute-start.4
  37.2 1.6 %collective-permute-done.4 = bf16[1536,128]{1,0:T(8,128)(2,1)S(1)} collective-permute-done((bf16[1536,128]{1,0:T(8,128)(2,1)S(1)}, bf16[1536,128]{1,0:T(8,128)(2,1)S(1)}, u32[]{:S(2)}, u32[]{:S(2)}) %collective-permute-start.4) | collective-permute-done | bytes 393248 | tf_op jit(solution)/shard_map/ppermute | solution.py:336
  38.8 0.1 add_convert_fusion
  38.9 16.2 %all_to_all.11.parts_ref = bf16[64,24,128]{2,1,0:T(8,128)(2,1)S(1)} all-to-all(bf16[64,24,128]{2,1,0:T(8,128)(2,1)S(1)} %bitcast.3), channel_id=1, replica_groups=mesh['seq'=4,'z'=4,'core'=2,'expert'=4] {'seq','z','expert'}, dimensions={0} | all-to-all | bytes 786432 | tf_op jit(solution)/shard_map/all_to_all | solution.py:338
  55.1 0.7 %finish.1 = (bf16[2,1536]{1,0:T(2,128)(2,1)}, bf16[2,1536]{1,0:T(2,128)(2,1)}) custom-call(bf16[64,24,128]{2,1,0:T(8,128)(2,1)S(1)} %all_to_all.11.parts_ref, f32[4,24,128]{2,1,0:T(8,128)S(1)} %get-tuple-element.16.mix_ref, bf16[2,1536]{1,0:T(2,128)(2,1)S(1)} %get-tuple-element.17.hid_ref), custom_call_target="tpu_custom_call" | custom-call | tf_op jit(solution)/shard_map/finish/pallas_call | solution.py:341
Async XLA Ops:
  0.6 9.1 %copy-start.6 = (f32[2,2]{1,0:T(2,128)S(1)}, f32[2,2]{1,0:T(2,128)}, u32[]{:S(2)}) copy-start(f32[2,2]{1,0:T(2,128)} %cw_hbm.1) | copy-start | bytes 52
  0.6 9.1 %copy-start.5 = (s32[2,2]{1,0:T(2,128)S(1)}, s32[2,2]{1,0:T(2,128)}, u32[]{:S(2)}) copy-start(s32[2,2]{1,0:T(2,128)} %ids_hbm.1) | copy-start | bytes 52
  0.7 9.0 %copy-start.4 = (f32[6144]{0:T(1024)S(1)}, f32[6144]{0:T(1024)}, u32[]{:S(2)}) copy-start(f32[6144]{0:T(1024)} %param.20) | copy-start | bytes 73732
  0.7 9.0 %copy-start.3 = (bf16[2,6144]{1,0:T(2,128)(2,1)S(1)}, bf16[2,6144]{1,0:T(2,128)(2,1)}, u32[]{:S(2)}) copy-start(bf16[2,6144]{1,0:T(2,128)(2,1)} %res_hbm.1) | copy-start | bytes 73732
  4.5 5.9 %collective-permute-start.2 = (bf16[112,128]{1,0:T(8,128)(2,1)S(1)}, bf16[112,128]{1,0:T(8,128)(2,1)S(1)}, u32[]{:S(2)}, u32[]{:S(2)}) collective-permute-start(bf16[112,128]{1,0:T(8,128)(2,1)S(1)} %attention.1.after.p0), channel_id=1, source_target_pairs={{0,64},{32,96},{64,0},{96,32},{1,65},{33,97},{65,1},{97,33},{2,66}... | collective-permute-start | bytes 86024 | tf_op jit(solution)/shard_map/ppermute | solution.py:302
  7.7 3.9 %collective-permute-start.1 = (bf16[112,128]{1,0:T(8,128)(2,1)S(1)}, bf16[112,128]{1,0:T(8,128)(2,1)S(1)}, u32[]{:S(2)}, u32[]{:S(2)}) collective-permute-start(bf16[112,128]{1,0:T(8,128)(2,1)S(1)} %attention.1.after.p0), channel_id=1, source_target_pairs={{0,96},{32,0},{64,32},{96,64},{1,97},{33,1},{65,33},{97,65},{2,98}... | collective-permute-start | bytes 86024 | tf_op jit(solution)/shard_map/ppermute | solution.py:302
  8.8 5.1 %collective-permute-start = (bf16[112,128]{1,0:T(8,128)(2,1)S(1)}, bf16[112,128]{1,0:T(8,128)(2,1)S(1)}, u32[]{:S(2)}, u32[]{:S(2)}) collective-permute-start(bf16[112,128]{1,0:T(8,128)(2,1)S(1)} %attention.1.after.p0), channel_id=1, source_target_pairs={{0,32},{32,64},{64,96},{96,0},{1,33},{33,65},{65,97},{97,1},{2,34}... | collective-permute-start | bytes 86024 | tf_op jit(solution)/shard_map/ppermute | solution.py:302
  13.9 19.5 %copy-start = (bf16[1,6144,512]{2,1,0:T(8,128)(2,1)S(1)}, bf16[1,6144,512]{2,1,0:T(8,128)(2,1)}, u32[]{:S(2)}) copy-start(bf16[1,6144,512]{2,1,0:T(8,128)(2,1)} %wg.1) | copy-start | bytes 18874372
  13.9 19.5 %copy-start.1 = (bf16[1,6144,512]{2,1,0:T(8,128)(2,1)S(1)}, bf16[1,6144,512]{2,1,0:T(8,128)(2,1)}, u32[]{:S(2)}) copy-start(bf16[1,6144,512]{2,1,0:T(8,128)(2,1)} %wu.1) | copy-start | bytes 18874372
  13.9 19.5 %copy-start.2 = (bf16[1,512,6144]{2,1,0:T(8,128)(2,1)S(1)}, bf16[1,512,6144]{2,1,0:T(8,128)(2,1)}, u32[]{:S(2)}) copy-start(bf16[1,512,6144]{2,1,0:T(8,128)(2,1)} %wd.1) | copy-start | bytes 18874372
  31.7 1.7 %collective-permute-start.3 = (bf16[16,96,128]{2,1,0:T(8,128)(2,1)S(1)}, bf16[16,96,128]{2,1,0:T(8,128)(2,1)S(1)}, u32[]{:S(2)}, u32[]{:S(2)}) collective-permute-start(bf16[16,96,128]{2,1,0:T(8,128)(2,1)S(1)} %all_to_all.10.xa), channel_id=1, source_target_pairs={{0,4},{4,0},{1,5},{5,1},{2,6},{6,2},{3,7},{7,3},{8,12},{12,8},{9,1... | collective-permute-start | bytes 1179656 | tf_op jit(solution)/shard_map/ppermute | solution.py:320
  37.0 1.8 %collective-permute-start.4 = (bf16[1536,128]{1,0:T(8,128)(2,1)S(1)}, bf16[1536,128]{1,0:T(8,128)(2,1)S(1)}, u32[]{:S(2)}, u32[]{:S(2)}) collective-permute-start(bf16[1536,128]{1,0:T(8,128)(2,1)S(1)} %get-tuple-element.15), channel_id=1, source_target_pairs={{0,4},{4,0},{1,5},{5,1},{2,6},{6,2},{3,7},{7,3},{8,12},{12,8},{9,1... | collective-permute-start | bytes 1179656 | tf_op jit(solution)/shard_map/ppermute | solution.py:336
